TPU v7x, 32 devices: a whole 2x2x4 slice. The times are simulated.
32 devices in a mesh: groups: 2 (over y), blk: 4 (over z), inner: 4 (over x, core).
Axes of the slice: x: 2, y: 2, z: 4, core: 2. Of those that a mesh axis runs over, the one named last changes fastest.
Arguments:
- tokens: bfloat16 [1536, 2048], P(('groups', 'blk'), 'inner'), parts along dimension 0, may hold values from -6 to 6
- out_grad: bfloat16 [1536, 2048], P(('groups', 'blk'), 'inner'), parts along dimension 0, may hold values from -0.29882812 to 0.29882812
- w_gate: bfloat16 [8192, 2048], P(('blk', 'inner')), may hold values from -0.125 to 0.125
- w_up: bfloat16 [8192, 2048], P(('blk', 'inner')), may hold values from -0.125 to 0.125
- w_down: bfloat16 [8192, 2048], P(('blk', 'inner')), may hold values from -0.0625 to 0.0625
Outputs:
- mixed: bfloat16 [1536, 2048], P(('groups', 'blk'), 'inner'), parts along dimension 0
- grad_gate: float32 [16384, 2048], P(('groups', 'blk', 'inner')), parts along dimension 0
- grad_up: float32 [16384, 2048], P(('groups', 'blk', 'inner')), parts along dimension 0
- grad_down: float32 [16384, 2048], P(('groups', 'blk', 'inner')), parts along dimension 0
There are 2 independent parts, one for each index of `groups`. A program takes and returns all parts, laid end to end along the dimension named above; an argument that names none is the same for every part. Nothing has to cross between parts.
All inputs are finite; a program needn't handle non-finite values.
Results may differ from a plain program's by a relative error of at most 0.0051.
Values may be sent and summed in bfloat16 or wider, within the bound.
A program may use at most 128 MiB of HBM per device.

v0:
```python
import jax
import jax.numpy as jnp
from jax import lax
from jax.sharding import PartitionSpec as P


def shifted(array, axis, by):
    count = lax.axis_size(axis)
    return lax.ppermute(array, axis, [(i, (i + by) % count) for i in range(count)])


def slab_rows(slab, rows):
    return lax.dot_general(slab, rows, (((1,), (1,)), ((), ())), preferred_element_type=jnp.float32)


def forward_term(rows, slab):
    gate_t = slab_rows(slab[0], rows)
    up_t = slab_rows(slab[1], rows)
    hidden = (jax.nn.silu(gate_t) * up_t).astype(jnp.bfloat16)
    return lax.dot_general(
        hidden, slab[2], (((0,), (0,)), ((), ())), preferred_element_type=jnp.float32
    )


def grad_term(rows, grads, slab):
    gate_t = slab_rows(slab[0], rows)
    up_t = slab_rows(slab[1], rows)
    sigma = jax.nn.sigmoid(gate_t)
    active = gate_t * sigma
    hidden = (active * up_t).astype(jnp.bfloat16)
    back = slab_rows(slab[2], grads)
    dgate = (back * up_t * sigma * (1.0 + gate_t * (1.0 - sigma))).astype(jnp.bfloat16)
    dup = (back * active).astype(jnp.bfloat16)
    gate_part = jnp.dot(dgate, rows, preferred_element_type=jnp.float32)
    up_part = jnp.dot(dup, rows, preferred_element_type=jnp.float32)
    down_part = jnp.dot(hidden, grads, preferred_element_type=jnp.float32)
    return jnp.stack([gate_part, up_part, down_part])


def on_device(tokens, out_grad, w_gate, w_up, w_down):
    rows, grads = (
        lax.all_gather(tokens, "inner", axis=1, tiled=True),
        lax.all_gather(out_grad, "inner", axis=1, tiled=True),
    )
    cycle_size = lax.axis_size("blk")
    own_slab = jnp.stack([w_gate, w_up, w_down])
    lagged = shifted(own_slab, "blk", 1)
    total = forward_term(rows, own_slab) + forward_term(rows, lagged)

    def advance(step, carry):
        current, acc = carry
        current = shifted(current, "blk", 1)
        return (current, acc + forward_term(rows, current))

    current, total = lax.fori_loop(0, cycle_size - 2, advance, (lagged, total))
    mixed = lax.psum_scatter(total, "inner", scatter_dimension=1, tiled=True).astype(jnp.bfloat16)
    carried = grad_term(rows, grads, own_slab)
    carried = shifted(carried.astype(jnp.bfloat16), "blk", 1).astype(carried.dtype)
    collected = carried + grad_term(rows, grads, lagged)
    return (mixed, collected[0], collected[1], collected[2])


def solution(mesh):
    return jax.shard_map(
        on_device,
        mesh=mesh,
        in_specs=(
            P(("groups", "blk"), "inner"),
            P(("groups", "blk"), "inner"),
            P(("blk", "inner"), None),
            P(("blk", "inner"), None),
            P(("blk", "inner"), None),
        ),
        out_specs=(
            P(("groups", "blk"), "inner"),
            P(("groups", "blk", "inner"), None),
            P(("groups", "blk", "inner"), None),
            P(("groups", "blk", "inner"), None),
        ),
        check_vma=False,
    )
```

profile of v0, /device:TPU:0, one launch (start us, length us, event | category | flops | bytes accessed | tf_op | source)
XLA Modules:
  0.0 626.9 jit_solution(1303332711188674524)
XLA Ops:
  7.2 6.8 %pad_maximum_fusion = bf16[3,512,2048]{2,1,0:T(8,128)(2,1)} fusion(bf16[1,512,2048]{2,1,0:T(8,128)(2,1)} %bitcast.78, bf16[1,512,2048]{2,1,0:T(8,128)(2,1)} %bitcast.80, bf16[1,512,2048]{2,1,0:T(8,128)(2,1)} %bitcast.79), kind=kLoop, calls=%fused_computation.10 | loop fusion | flops 6291456 | bytes 12582912 | tf_op jit(solution)/shard_map/stack | solution.py:46
  14.1 3.0 collective-permute-start.1
  17.1 8.6 %all_gather.6 = bf16[192,2048]{1,0:T(8,128)(2,1)S(1)} all-gather(bf16[192,512]{1,0:T(8,128)(2,1)S(1)} %copy-done.8), channel_id=1, replica_groups=mesh['groups'=2,'blk'=4,'inner'=4] {'inner'}, dimensions={1}, use_global_device_ids=true | all-gather | bytes 983040 | tf_op jit(solution)/shard_map/all_gather | solution.py:42
  25.7 8.7 %all_gather.7 = bf16[192,2048]{1,0:T(8,128)(2,1)S(1)} all-gather(bf16[192,512]{1,0:T(8,128)(2,1)S(1)} %copy-done.9), channel_id=1, replica_groups=mesh['groups'=2,'blk'=4,'inner'=4] {'inner'}, dimensions={1}, use_global_device_ids=true | all-gather | bytes 983040 | tf_op jit(solution)/shard_map/all_gather | solution.py:43
  39.5 3.2 pad_maximum_fusion.1
  44.9 110.9 %collective-permute-done.1 = bf16[3,512,2048]{2,1,0:T(8,128)(2,1)} collective-permute-done((bf16[3,512,2048]{2,1,0:T(8,128)(2,1)}, bf16[3,512,2048]{2,1,0:T(8,128)(2,1)}, u32[]{:S(2)}, u32[]{:S(2)}) %collective-permute-start.1) | collective-permute-done | bytes 6291488 | tf_op jit(solution)/shard_map/ppermute | solution.py:9
  155.8 6.6 %copy.10 = bf16[3,512,2048]{2,1,0:T(8,128)(2,1)} copy(bf16[3,512,2048]{2,1,0:T(8,128)(2,1)} %collective-permute-done.1) | data formatting | bytes 12582912
  162.4 2.4 fusion.8
  164.8 3.2 multiply_convert_fusion.6
  168.0 2.3 convolution_add_fusion.1
  170.3 420.6 %while.12 = (s32[]{:T(128)}, bf16[3,512,2048]{2,1,0:T(8,128)(2,1)}, f32[192,2048]{1,0:T(8,128)S(1)}, bf16[192,2048]{1,0:T(8,128)(2,1)S(1)}, s32[]{:T(128)}) while((s32[]{:T(128)}, bf16[3,512,2048]{2,1,0:T(8,128)(2,1)}, f32[192,2048]{1,0:T(8,128)S(1)}, bf16[192,2048]{1,0:T(8,128)(2,1)S(1)}, s32[]{:T(128)}) %tuple.26), condition=%wide.region_1.2_spmd, body=%wide.region_0.1_spmd.sunk | while | flops 1208942592 | bytes 49545316 | solution.py:55
  170.4 254.2 %collective-permute-done = bf16[3,512,2048]{2,1,0:T(8,128)(2,1)} collective-permute-done((bf16[3,512,2048]{2,1,0:T(8,128)(2,1)}, bf16[3,512,2048]{2,1,0:T(8,128)(2,1)}, u32[]{:S(2)}, u32[]{:S(2)}) %collective-permute-start) | collective-permute-done | bytes 6291488 | tf_op jit(solution)/shard_map/while/body/eval_jaxpr/ppermute | solution.py:9
  424.6 6.6 %copy.16 = bf16[3,512,2048]{2,1,0:T(8,128)(2,1)} copy(bf16[3,512,2048]{2,1,0:T(8,128)(2,1)} %collective-permute-done) | data formatting | bytes 12582912 | tf_op jit(solution)/shard_map/while
  431.2 3.2 fusion.50
  434.4 3.9 convolution_add_fusion.3
  438.4 138.8 %collective-permute-done = bf16[3,512,2048]{2,1,0:T(8,128)(2,1)} collective-permute-done((bf16[3,512,2048]{2,1,0:T(8,128)(2,1)}, bf16[3,512,2048]{2,1,0:T(8,128)(2,1)}, u32[]{:S(2)}, u32[]{:S(2)}) %collective-permute-start) | collective-permute-done | bytes 6291488 | tf_op jit(solution)/shard_map/while/body/eval_jaxpr/ppermute | solution.py:9
  577.2 6.6 %copy.16 = bf16[3,512,2048]{2,1,0:T(8,128)(2,1)} copy(bf16[3,512,2048]{2,1,0:T(8,128)(2,1)} %collective-permute-done) | data formatting | bytes 12582912 | tf_op jit(solution)/shard_map/while
  583.8 3.2 fusion.50
  587.0 3.9 convolution_add_fusion.3
  593.8 2.4 fusion.9
  598.1 8.1 %maximum_add_fusion = f32[3,512,2048]{2,1,0:T(8,128)} fusion(f32[1,512,2048]{2,1,0:T(8,128)S(1)} %convolution_bitcast_fusion, f32[1,512,2048]{2,1,0:T(8,128)S(1)} %convolution_bitcast_fusion.1, f32[1,512,2048]{2,1,0:T(8,128)S(1)} %convolution_bitcast_fusion.2, bf16[3,512,2048]{2,1,0:T(8,128)(2,1)} %collective-permute-done.2), kind=kLoop, calls=%fused_computation.9 | loop fusion | flops 12582912 | bytes 31457280 | tf_op jit(solution)/shard_map/add | solution.py:59
  606.2 10.0 %slice_bitcast_fusion.10 = (f32[512,2048]{1,0:T(8,128)}, f32[512,2048]{1,0:T(8,128)}, f32[512,2048]{1,0:T(8,128)}) fusion(f32[3,512,2048]{2,1,0:T(8,128)} %maximum_add_fusion), kind=kLoop, calls=%fused_computation.12 | loop fusion | bytes 25165824 | tf_op jit(solution)/shard_map/squeeze | solution.py:60
  616.2 2.2 reduce-scatter.2.cloned.1.call-done
  618.4 1.7 convert_element_type.32
  (36 shorter events, 12.1 us)
Async XLA Ops:
  7.2 611.2 %reduce-scatter.2.cloned.1.call-start = ((), (), s32[]{:S(2)}) async-start(), calls=%async_computation.1 | async-start | bytes 1966080 | tf_op jit(solution)/shard_map/reduce_scatter | solution.py:56
  7.2 9.9 %copy-start.8 = (bf16[192,512]{1,0:T(8,128)(2,1)S(1)}, bf16[192,512]{1,0:T(8,128)(2,1)}, u32[]{:S(2)}) copy-start(bf16[192,512]{1,0:T(8,128)(2,1)} %param.7) | copy-start | bytes 589828
  7.2 18.5 %copy-start.9 = (bf16[192,512]{1,0:T(8,128)(2,1)S(1)}, bf16[192,512]{1,0:T(8,128)(2,1)}, u32[]{:S(2)}) copy-start(bf16[192,512]{1,0:T(8,128)(2,1)} %param.8) | copy-start | bytes 589828
  7.2 27.2 %copy-start.4 = (bf16[512,2048]{1,0:T(8,128)(2,1)S(1)}, bf16[512,2048]{1,0:T(8,128)(2,1)}, u32[]{:S(2)}) copy-start(bf16[512,2048]{1,0:T(8,128)(2,1)} %param.9) | copy-start | bytes 6291460
  14.1 21.2 %copy-start.5 = (bf16[512,2048]{1,0:T(8,128)(2,1)S(1)}, bf16[512,2048]{1,0:T(8,128)(2,1)}, u32[]{:S(2)}) copy-start(bf16[512,2048]{1,0:T(8,128)(2,1)} %param.10) | copy-start | bytes 6291460
  14.1 141.7 %collective-permute-start.1 = (bf16[3,512,2048]{2,1,0:T(8,128)(2,1)}, bf16[3,512,2048]{2,1,0:T(8,128)(2,1)}, u32[]{:S(2)}, u32[]{:S(2)}) collective-permute-start(bf16[3,512,2048]{2,1,0:T(8,128)(2,1)} %pad_maximum_fusion), channel_id=1, source_target_pairs={{0,4},{4,8},{8,12},{12,0},{1,5},{5,9},{9,13},{13,1},{2,6},{6,10},{... | collective-permute-start | bytes 18874376 | tf_op jit(solution)/shard_map/ppermute | solution.py:9
  34.4 2.5 copy-start.1
  35.2 1.7 copy-start
  42.7 555.4 %collective-permute-start.2 = (bf16[3,512,2048]{2,1,0:T(8,128)(2,1)}, bf16[3,512,2048]{2,1,0:T(8,128)(2,1)}, u32[]{:S(2)}, u32[]{:S(2)}) collective-permute-start(bf16[3,512,2048]{2,1,0:T(8,128)(2,1)} %pad_maximum_fusion.1), channel_id=1, source_target_pairs={{0,4},{4,8},{8,12},{12,0},{1,5},{5,9},{9,13},{13,1},{2,6},{6,10},{... | collective-permute-start | bytes 18874376 | tf_op jit(solution)/shard_map/ppermute | solution.py:9
  168.0 2.3 copy-start.6
  170.3 421.8 %copy-start.2 = (bf16[192,2048]{1,0:T(8,128)(2,1)S(1)}, bf16[192,2048]{1,0:T(8,128)(2,1)}, u32[]{:S(2)}) copy-start(bf16[192,2048]{1,0:T(8,128)(2,1)} %copy-done.1) | copy-start | bytes 2359300
  170.3 254.3 %collective-permute-start = (bf16[3,512,2048]{2,1,0:T(8,128)(2,1)}, bf16[3,512,2048]{2,1,0:T(8,128)(2,1)}, u32[]{:S(2)}, u32[]{:S(2)}) collective-permute-start(bf16[3,512,2048]{2,1,0:T(8,128)(2,1)} %get-tuple-element.73), channel_id=1, source_target_pairs={{0,4},{4,8},{8,12},{12,0},{1,5},{5,9},{9,13},{13,1},{2,6},{6,10},{... | collective-permute-start | bytes 18874376 | tf_op jit(solution)/shard_map/while/body/eval_jaxpr/ppermute | solution.py:9
  438.3 138.9 %collective-permute-start = (bf16[3,512,2048]{2,1,0:T(8,128)(2,1)}, bf16[3,512,2048]{2,1,0:T(8,128)(2,1)}, u32[]{:S(2)}, u32[]{:S(2)}) collective-permute-start(bf16[3,512,2048]{2,1,0:T(8,128)(2,1)} %get-tuple-element.73), channel_id=1, source_target_pairs={{0,4},{4,8},{8,12},{12,0},{1,5},{5,9},{9,13},{13,1},{2,6},{6,10},{... | collective-permute-start | bytes 18874376 | tf_op jit(solution)/shard_map/while/body/eval_jaxpr/ppermute | solution.py:9
  590.9 1.2 copy-start.3
  596.2 1.0 copy-start.7
Sparse Core Ops, SparseCore 0:
  592.2 26.1 reduce-scatter.1
where the time goes:
time: 628 us; the launch traced here: 627 us
  waiting for transfers between devices  506 us (81%)
  matrix products  33.4 us (5%)
  local copies, waits for them, and re-layouts  31.2 us (5%)
  other arithmetic  19.9 us (3%)
  blocking collectives  17.3 us (3%)
  between operations  14.2 us (2%)
    ppermute x4, waiting for transfers between devices, shifted(): lax.ppermute(array, axis, [(i, (i + by) % count) for i in range(count)])  504 us
    dot_general x8, matrix products, slab_rows(): lax.dot_general(slab, rows, (((1,), (1,)), ((), ())), preferred_element_t...  17 us
    while x2, local copies, waits for them, and re-layouts  13.2 us
  transfers between devices with their start and end apart: 5, of which 4 were waited for; matrix products, arithmetic and copies ran while one was open for 12% of the time, Pallas kernels for 0%

commit v1 on v0

v1 whole, which is shorter than its diff:
```python
import jax
import jax.numpy as jnp
from jax import lax
from jax.sharding import PartitionSpec as P

BF = jnp.bfloat16
F32 = jnp.float32


def shifted(array, axis, by):
    count = lax.axis_size(axis)
    return lax.ppermute(array, axis, [(i, (i + by) % count) for i in range(count)])


def nt(a, b):
    return lax.dot_general(a, b, (((1,), (1,)), ((), ())), preferred_element_type=F32)


def tn(a, b):
    return lax.dot_general(a, b, (((0,), (0,)), ((), ())), preferred_element_type=F32)


def on_device(tokens, out_grad, w_gate, w_up, w_down):
    n = lax.axis_size("blk")
    b = lax.axis_index("blk")
    rows = tokens.shape[0]

    y_prev = shifted(out_grad, "blk", 1)
    y_next = shifted(out_grad, "blk", -1)
    x_cols = lax.all_gather(tokens, "blk", axis=0, tiled=True)
    x = lax.all_gather(x_cols, "inner", axis=1, tiled=True)
    y = lax.all_gather(
        jnp.concatenate([y_prev, out_grad, y_next], axis=0), "inner", axis=1, tiled=True
    )

    def block(array, index):
        return lax.dynamic_slice_in_dim(array, (index % n) * rows, rows, 0)

    def pair(array, first):
        return jnp.concatenate([block(array, first), block(array, first + 1)], axis=0)

    gate = nt(x, w_gate)
    up = nt(x, w_up)
    hidden = (jax.nn.silu(gate) * up).astype(BF)

    gate_2 = pair(gate, b)
    up_2 = pair(up, b)
    hidden_2 = pair(hidden, b)
    back = nt(y[rows:], w_down)
    sigma = jax.nn.sigmoid(gate_2)
    dgate = (back * up_2 * sigma * (1.0 + gate_2 * (1.0 - sigma))).astype(BF)
    dup = (back * gate_2 * sigma).astype(BF)
    moved = shifted(jnp.stack([dgate, dup, hidden_2]), "blk", 1)

    partial = jnp.dot(hidden, w_down, preferred_element_type=F32).astype(BF)
    mixed = lax.psum_scatter(partial, "inner", scatter_dimension=1, tiled=True)
    mixed = lax.psum_scatter(mixed, "blk", scatter_dimension=0, tiled=True).astype(BF)

    x_2 = pair(x, b - 1 + n)
    y_2 = y[: 2 * rows]
    return (mixed, tn(moved[0], x_2), tn(moved[1], x_2), tn(moved[2], y_2))


def solution(mesh):
    return jax.shard_map(
        on_device,
        mesh=mesh,
        in_specs=(
            P(("groups", "blk"), "inner"),
            P(("groups", "blk"), "inner"),
            P(("blk", "inner"), None),
            P(("blk", "inner"), None),
            P(("blk", "inner"), None),
        ),
        out_specs=(
            P(("groups", "blk"), "inner"),
            P(("groups", "blk", "inner"), None),
            P(("groups", "blk", "inner"), None),
            P(("groups", "blk", "inner"), None),
        ),
        check_vma=False,
    )
```

time: 628 us -> 157 us (0.25)
  waiting for transfers between devices: 506 us -> 86 us
  local copies, waits for them, and re-layouts: 31.2 us -> 4.03 us
  other arithmetic: 19.9 us -> 2.04 us
  matrix products: 33.4 us -> 23.8 us
    ppermute x4 -> x3, waiting for transfers between devices: 504 us -> 4.6 us  [shifted(): lax.ppermute(array, axis, [(i, (i + by) % count) for i in range(count)])]
    reduce_scatter x1 -> x2, waiting for transfers between devices: 2.21 us -> 50.4 us  [the longest x1 35.7 us: on_device(): mixed = lax.psum_scatter(partial, 'inner', scatter_dimension=1, tiled=True)]
    all_gather x0 -> x2, waiting for transfers between devices: none -> 30.9 us  [the longest x1 19 us: on_device(): x = lax.all_gather(x_cols, 'inner', axis=1, tiled=True)]
    while x2 -> x0, local copies, waits for them, and re-layouts: 13.2 us -> none
    squeeze x1 -> x0, local copies, waits for them, and re-layouts: 9.97 us -> none  [on_device(): return (mixed, collected[0], collected[1], collected[2])]
    dot_general x18 -> x7, matrix products: 33.4 us -> 23.8 us  [the longest x3 10.4 us: nt(): lax.dot_general(a, b, (((1,), (1,)), ((), ())), preferred_element_type=F32)]
    another operation x2, other arithmetic: 10.1 us -> 1.17 us  [on_device(): moved = shifted(jnp.stack([dgate, dup, hidden_2]), 'blk', 1)]
    add x1 -> x0, other arithmetic: 8.12 us -> none  [on_device(): collected = carried + grad_term(rows, grads, lagged)]
  transfers between devices with their start and end apart: 5 -> 7, of which waited for: 4 -> 6; matrix products, arithmetic and copies ran while one was open for 12% -> 19% of each run, Pallas kernels for 0% -> 0%
where the time goes in v1:
time: 157 us
  waiting for transfers between devices  86 us (55%)
  matrix products  23.8 us (15%)
  blocking collectives  21.9 us (14%)
  between operations  13.9 us (9%)
  starting transfers between devices  5.52 us (4%)
  local copies, waits for them, and re-layouts  4.03 us (3%)
  other arithmetic  2.04 us (1%)
    reduce_scatter x1, waiting for transfers between devices, on_device(): mixed = lax.psum_scatter(partial, 'inner', scatter_dimension=1, tiled=True)  35.7 us
    all_gather x1, blocking collectives, on_device(): x_cols = lax.all_gather(tokens, 'blk', axis=0, tiled=True)  21.9 us
    all_gather x1, waiting for transfers between devices, on_device(): x = lax.all_gather(x_cols, 'inner', axis=1, tiled=True)  19 us
    reduce_scatter x1, waiting for transfers between devices, on_device(): lax.psum_scatter(mixed, 'blk', scatter_dimension=0, tiled=True).astype(BF)  14.7 us
    all_gather x1, waiting for transfers between devices, on_device(): lax.all_gather(jnp.concatenate([y_prev, out_grad, y_next], axis=0), 'inne...  11.9 us
    dot_general x3, matrix products, nt(): lax.dot_general(a, b, (((1,), (1,)), ((), ())), preferred_element_type=F32)  10.4 us
    dot_general x3, matrix products, tn(): lax.dot_general(a, b, (((0,), (0,)), ((), ())), preferred_element_type=F32)  9.95 us
    ppermute x3, starting transfers between devices, shifted(): lax.ppermute(array, axis, [(i, (i + by) % count) for i in range(count)])  5.36 us
  transfers between devices with their start and end apart: 7, of which 6 were waited for; matrix products, arithmetic and copies ran while one was open for 19% of the time, Pallas kernels for 0%

profile of v1, /device:TPU:0, one launch (start us, length us, event | category | flops | bytes accessed | tf_op | source)
XLA Modules:
  0.0 157.2 jit_solution(10959887135574146709)
XLA Ops:
  7.2 21.9 %all_gather.9 = bf16[768,512]{1,0:T(8,128)(2,1)} all-gather(bf16[192,512]{1,0:T(8,128)(2,1)} %param.5), channel_id=1, replica_groups=mesh['groups'=2,'blk'=4,'inner'=4] {'blk'}, dimensions={0}, use_global_device_ids=true | all-gather | bytes 983040 | tf_op jit(solution)/shard_map/all_gather | solution.py:30
  29.2 0.2 collective-permute-start
  29.4 3.7 %collective-permute-start.1 = (bf16[192,512]{1,0:T(8,128)(2,1)S(1)}, bf16[192,512]{1,0:T(8,128)(2,1)S(1)}, u32[]{:S(2)}, u32[]{:S(2)}) collective-permute-start(bf16[192,512]{1,0:T(8,128)(2,1)S(1)} %copy-done.5), channel_id=1, source_target_pairs={{0,12},{4,0},{8,4},{12,8},{1,13},{5,1},{9,5},{13,9},{2,14},{6,2},{... | collective-permute-start | bytes 589832 | tf_op jit(solution)/shard_map/ppermute | solution.py:12
  33.1 4.4 %collective-permute-done = bf16[192,512]{1,0:T(8,128)(2,1)S(1)} collective-permute-done((bf16[192,512]{1,0:T(8,128)(2,1)S(1)}, bf16[192,512]{1,0:T(8,128)(2,1)S(1)}, u32[]{:S(2)}, u32[]{:S(2)}) %collective-permute-start) | collective-permute-done | bytes 196640 | tf_op jit(solution)/shard_map/ppermute | solution.py:12
  37.5 0.2 collective-permute-done.1
  37.7 0.9 pad_maximum_fusion.5
  38.6 0.0 reduce-scatter.3.cloned.1.call-start
  38.6 19.0 %all-gather.3.cloned.1.call-done = bf16[768,2048]{1,0:T(8,128)(2,1)} async-done(((bf16[768,512]{1,0:T(8,128)(2,1)}), bf16[768,2048]{1,0:T(8,128)(2,1)}) %all-gather.3.cloned.1.call-update) | async-done | bytes 3145744 | tf_op jit(solution)/shard_map/all_gather | solution.py:31
  57.7 4.5 %fusion.15 = f32[768,512]{1,0:T(8,128)S(1)} fusion(bf16[768,2048]{1,0:T(8,128)(2,1)} %all-gather.3.cloned.1.call-done, bf16[512,2048]{1,0:T(8,128)(2,1)} %param.7), kind=kOutput, calls=%fused_computation.34 | convolution fusion | flops 1610612736 | bytes 6815744 | tf_op jit(solution)/shard_map/dot_general | solution.py:16
  62.2 3.1 %multiply_convert_fusion = (bf16[768,512]{1,0:T(8,128)(2,1)S(1)}, f32[768,512]{1,0:T(8,128)}) fusion(f32[768,512]{1,0:T(8,128)S(1)} %fusion.15, bf16[768,2048]{1,0:T(8,128)(2,1)S(1)} %copy-done.2, bf16[512,2048]{1,0:T(8,128)(2,1)S(1)} %copy-done.6), kind=kOutput, calls=%fused_computation.6 | convolution fusion | flops 1612972032 | bytes 9175040 | tf_op jit(solution)/shard_map/dot_general | solution.py:16
  65.3 3.5 %convolution_convert_fusion = bf16[768,2048]{1,0:T(8,128)(2,1)} fusion(bf16[768,512]{1,0:T(8,128)(2,1)S(1)} %get-tuple-element.14, bf16[512,2048]{1,0:T(8,128)(2,1)S(1)} %copy-done), kind=kOutput, calls=%fused_computation | convolution fusion | flops 1612185600 | bytes 6029312 | tf_op jit(solution)/shard_map/dot_general | solution.py:55
  69.0 1.3 constant_dynamic-slice_fusion.5
  70.2 0.3 copy-done.3
  70.5 0.9 constant_dynamic-slice_fusion.7
  71.5 11.9 %all-gather.5.cloned.1.call-done = bf16[576,2048]{1,0:T(8,128)(2,1)} async-done(((bf16[576,512]{1,0:T(8,128)(2,1)}), bf16[576,2048]{1,0:T(8,128)(2,1)}) %all-gather.5.cloned.1.call-update) | async-done | bytes 2359312 | tf_op jit(solution)/shard_map/all_gather | solution.py:32
  83.4 2.8 %fusion.10 = (bf16[1,384,512]{2,1,0:T(8,128)(2,1)S(1)}, bf16[1,384,512]{2,1,0:T(8,128)(2,1)S(1)}) fusion(f32[192,512]{1,0:T(8,128)S(1)} %get-tuple-element.11, f32[192,512]{1,0:T(8,128)S(1)} %get-tuple-element.10, f32[192,512]{1,0:T(8,128)} %get-tuple-element.9, f32[192,512]{1,0:T(8,128)} %get-tuple-element.8, bf16[512,2048]{1,0:T(8,128)(2,1)S(1)} %copy-done, ...), kind=kOutput, calls=%fused_computation.23 | convolution fusion | flops 808255488 | bytes 6029312 | tf_op jit(solution)/shard_map/dot_general | solution.py:16
  86.2 1.1 pad_maximum_fusion.1
  87.3 1.5 collective-permute-start.2
  88.8 35.7 %reduce-scatter.3.cloned.1.call-done = bf16[768,512]{1,0:T(8,128)(2,1)} async-done(((bf16[768,2048]{1,0:T(8,128)(2,1)}), bf16[768,512]{1,0:T(8,128)(2,1)}) %reduce-scatter.3.cloned.1.call-update) | async-done | bytes 786448 | tf_op jit(solution)/shard_map/reduce_scatter | solution.py:56
  124.5 1.5 constant_dynamic-slice_fusion.1
  126.0 3.3 %fusion.4 = f32[512,2048]{1,0:T(8,128)} fusion(bf16[192,2048]{1,0:T(8,128)(2,1)S(1)} %get-tuple-element.5, bf16[192,2048]{1,0:T(8,128)(2,1)S(1)} %get-tuple-element.4, bf16[3,384,512]{2,1,0:T(8,128)(2,1)S(1)} %collective-permute-done.2), kind=kOutput, calls=%fused_computation.8 | convolution fusion | flops 808452096 | bytes 6160384 | tf_op jit(solution)/shard_map/dot_general | solution.py:20
  129.3 3.3 %fusion.5 = f32[512,2048]{1,0:T(8,128)} fusion(bf16[192,2048]{1,0:T(8,128)(2,1)S(1)} %get-tuple-element.5, bf16[192,2048]{1,0:T(8,128)(2,1)S(1)} %get-tuple-element.4, bf16[3,384,512]{2,1,0:T(8,128)(2,1)S(1)} %collective-permute-done.2), kind=kOutput, calls=%fused_computation.9 | convolution fusion | flops 808452096 | bytes 6160384 | tf_op jit(solution)/shard_map/dot_general | solution.py:20
  132.7 3.3 %fusion = f32[512,2048]{1,0:T(8,128)} fusion(bf16[576,2048]{1,0:T(8,128)(2,1)S(1)} %copy-done.1, bf16[3,384,512]{2,1,0:T(8,128)(2,1)S(1)} %collective-permute-done.2), kind=kOutput, calls=%fused_computation.1 | convolution fusion | flops 805306368 | bytes 6160384 | tf_op jit(solution)/shard_map/dot_general | solution.py:20
  136.0 14.7 %reduce-scatter.5.cloned.1.call-done = bf16[192,512]{1,0:T(8,128)(2,1)} async-done(((bf16[768,512]{1,0:T(8,128)(2,1)}), bf16[192,512]{1,0:T(8,128)(2,1)}) %reduce-scatter.5.cloned.1.call-update) | async-done | bytes 196624 | tf_op jit(solution)/shard_map/reduce_scatter | solution.py:57
  (23 shorter events, 0.3 us)
Async XLA Ops:
  7.2 58.1 %copy-start = (bf16[512,2048]{1,0:T(8,128)(2,1)S(1)}, bf16[512,2048]{1,0:T(8,128)(2,1)}, u32[]{:S(2)}) copy-start(bf16[512,2048]{1,0:T(8,128)(2,1)} %param.9) | copy-start | bytes 6291460
  7.2 22.0 %copy-start.5 = (bf16[192,512]{1,0:T(8,128)(2,1)S(1)}, bf16[192,512]{1,0:T(8,128)(2,1)}, u32[]{:S(2)}) copy-start(bf16[192,512]{1,0:T(8,128)(2,1)} %param.6) | copy-start | bytes 589828
  7.2 50.5 %all-gather.3.cloned.1.call-start = ((), (), s32[]{:S(2)}) async-start(), calls=%async_computation.2 | async-start | bytes 3932160 | tf_op jit(solution)/shard_map/all_gather | solution.py:31
  29.2 54.2 %all-gather.5.cloned.1.call-start = ((), (), s32[]{:S(2)}) async-start(), calls=%async_computation.5 | async-start | bytes 2949120 | tf_op jit(solution)/shard_map/all_gather | solution.py:32
  29.2 8.3 %collective-permute-start = (bf16[192,512]{1,0:T(8,128)(2,1)S(1)}, bf16[192,512]{1,0:T(8,128)(2,1)S(1)}, u32[]{:S(2)}, u32[]{:S(2)}) collective-permute-start(bf16[192,512]{1,0:T(8,128)(2,1)S(1)} %copy-done.5), channel_id=1, source_target_pairs={{0,4},{4,8},{8,12},{12,0},{1,5},{5,9},{9,13},{13,1},{2,6},{6,10},{... | collective-permute-start | bytes 589832 | tf_op jit(solution)/shard_map/ppermute | solution.py:12
  29.4 8.3 %collective-permute-start.1 = (bf16[192,512]{1,0:T(8,128)(2,1)S(1)}, bf16[192,512]{1,0:T(8,128)(2,1)S(1)}, u32[]{:S(2)}, u32[]{:S(2)}) collective-permute-start(bf16[192,512]{1,0:T(8,128)(2,1)S(1)} %copy-done.5), channel_id=1, source_target_pairs={{0,12},{4,0},{8,4},{12,8},{1,13},{5,1},{9,5},{13,9},{2,14},{6,2},{... | collective-permute-start | bytes 589832 | tf_op jit(solution)/shard_map/ppermute | solution.py:12
  38.6 85.9 %reduce-scatter.3.cloned.1.call-start = ((), (), s32[]{:S(2)}) async-start(), calls=%async_computation.3 | async-start | bytes 3932160 | tf_op jit(solution)/shard_map/reduce_scatter | solution.py:56
  57.7 4.5 %copy-start.2 = (bf16[768,2048]{1,0:T(8,128)(2,1)S(1)}, bf16[768,2048]{1,0:T(8,128)(2,1)}, u32[]{:S(2)}) copy-start(bf16[768,2048]{1,0:T(8,128)(2,1)} %all-gather.3.cloned.1.call-done) | copy-start | bytes 9437188
  57.7 4.5 %copy-start.6 = (bf16[512,2048]{1,0:T(8,128)(2,1)S(1)}, bf16[512,2048]{1,0:T(8,128)(2,1)}, u32[]{:S(2)}) copy-start(bf16[512,2048]{1,0:T(8,128)(2,1)} %param.8) | copy-start | bytes 6291460
  62.2 3.1 %copy-start.4 = (f32[768,512]{1,0:T(8,128)}, f32[768,512]{1,0:T(8,128)S(1)}, u32[]{:S(2)}) copy-start(f32[768,512]{1,0:T(8,128)S(1)} %fusion.15) | copy-start | bytes 4718596
  68.8 81.8 %reduce-scatter.5.cloned.1.call-start = ((), (), s32[]{:S(2)}) async-start(), calls=%async_computation.4 | async-start | bytes 983040 | tf_op jit(solution)/shard_map/reduce_scatter | solution.py:57
  68.9 1.6 %copy-start.3 = (f32[768,512]{1,0:T(8,128)S(1)}, f32[768,512]{1,0:T(8,128)}, u32[]{:S(2)}) copy-start(f32[768,512]{1,0:T(8,128)} %get-tuple-element.15) | copy-start | bytes 4718596
  87.3 38.7 %collective-permute-start.2 = (bf16[3,384,512]{2,1,0:T(8,128)(2,1)}, bf16[3,384,512]{2,1,0:T(8,128)(2,1)S(1)}, u32[]{:S(2)}, u32[]{:S(2)}) collective-permute-start(bf16[3,384,512]{2,1,0:T(8,128)(2,1)} %pad_maximum_fusion.1), channel_id=1, source_target_pairs={{0,4},{4,8},{8,12},{12,0},{1,5},{5,9},{9,13},{13,1},{2,6},{6,10},{... | collective-permute-start | bytes 3538952 | tf_op jit(solution)/shard_map/ppermute | solution.py:12
  129.3 3.3 %copy-start.1 = (bf16[576,2048]{1,0:T(8,128)(2,1)S(1)}, bf16[576,2048]{1,0:T(8,128)(2,1)}, u32[]{:S(2)}) copy-start(bf16[576,2048]{1,0:T(8,128)(2,1)} %all-gather.5.cloned.1.call-done) | copy-start | bytes 7077892
Sparse Core Ops, SparseCore 0:
  29.3 28.3 all-gather.2
  59.2 24.0 all-gather.4
  86.5 37.9 reduce-scatter.2
  127.3 23.3 reduce-scatter.4

commit v2 on v1

--- a/solution.py
+++ b/solution.py
@@ -1,6 +1,10 @@
+import functools
+
 import jax
 import jax.numpy as jnp
 from jax import lax
+from jax.experimental import pallas as pl
+from jax.experimental.pallas import tpu as pltpu
 from jax.sharding import PartitionSpec as P
 
 BF = jnp.bfloat16
@@ -61,9 +65,247 @@
     return (mixed, tn(moved[0], x_2), tn(moved[1], x_2), tn(moved[2], y_2))
 
 
+MESH = pl.DeviceIdType.MESH
+
+
+def places():
+    z = lax.axis_index("blk")
+    i = lax.axis_index("inner")
+    x, c = i // 2, lax.rem(i, 2)
+    return z, i, (1 - x) * 2 + c, x * 2 + (1 - c), (1 - x) * 2 + (1 - c)
+
+
+def greet(z, i, n, ix, ic):
+    barrier = pltpu.get_barrier_semaphore()
+    for k in range(1, n):
+        pl.semaphore_signal(
+            barrier, inc=1, device_id={"blk": lax.rem(z + k, n), "inner": i}, device_id_type=MESH
+        )
+    for other in (ix, ic):
+        pl.semaphore_signal(
+            barrier, inc=1, device_id={"blk": z, "inner": other}, device_id_type=MESH
+        )
+    pl.semaphore_wait(barrier, n + 1)
+
+
+def gather_kernel(n, t_ref, g_ref, x_ref, y_ref, zsend, send, recv):
+    z, i, ix, ic, ixc = places()
+    cols = t_ref.shape[1]
+
+    def view(item, inner):
+        ref, slot, _ = item
+        return ref.at[slot, :, pl.ds(pl.multiple_of(inner * cols, cols), cols)]
+
+    def copy(src, dst, ssem, rsem, blk, inner):
+        return pltpu.make_async_remote_copy(
+            src_ref=src, dst_ref=dst, send_sem=ssem, recv_sem=rsem,
+            device_id={"blk": blk, "inner": inner}, device_id_type=MESH,
+        )
+
+    greet(z, i, n, ix, ic)
+
+    def x_item(k):
+        slot = lax.rem(z + k, n)
+        return (x_ref, slot, slot)
+
+    def y_item(slot):
+        return (y_ref, slot, n + slot)
+
+    own_x, own_y = x_item(0), y_item(1)
+    z_copies = []
+
+    def z_send(src, item, blk):
+        q = item[2]
+        made = copy(src, view(item, i), zsend.at[len(z_copies)], recv.at[q, 0], blk, i)
+        made.start()
+        z_copies.append(made)
+
+    up, down = lax.rem(z + 1, n), lax.rem(z + n - 1, n)
+    z_send(t_ref, own_x, up)
+    z_send(t_ref, own_x, down)
+    for k in range(2, n - 1):
+        z_send(t_ref, own_x, lax.rem(z + k, n))
+    z_send(g_ref, y_item(2), down)
+    z_send(g_ref, y_item(0), up)
+    here = pl.ds(pl.multiple_of(i * cols, cols), cols)
+    x_ref[z, :, here] = t_ref[...]
+    y_ref[1, :, here] = g_ref[...]
+
+    items = [own_x, own_y, x_item(1), x_item(n - 1), y_item(2)]
+    items += [x_item(k) for k in range(2, n - 1)] + [y_item(0)]
+    sent = []
+
+    def second(item):
+        q = item[2]
+        v = view(item, ix)
+        copy(v, v, send.at[q, 1], recv.at[q, 1], z, ix).wait_recv()
+        made = copy(v, v, send.at[q, 2], recv.at[q, 3], z, ic)
+        made.start()
+        sent.append(made)
+
+    for at, item in enumerate(items):
+        q = item[2]
+        v = view(item, i)
+        if at >= 2:
+            copy(v, v, send.at[q, 0], recv.at[q, 0], z, ix).wait_recv()
+        made = copy(v, v, send.at[q, 0], recv.at[q, 1], z, ix)
+        made.start()
+        sent.append(made)
+        made = copy(v, v, send.at[q, 1], recv.at[q, 2], z, ic)
+        made.start()
+        sent.append(made)
+        if at >= 1:
+            second(items[at - 1])
+    second(items[-1])
+    for item in items:
+        q = item[2]
+        v = view(item, ic)
+        copy(v, v, send.at[q, 1], recv.at[q, 2], z, ic).wait_recv()
+        v = view(item, ixc)
+        copy(v, v, send.at[q, 2], recv.at[q, 3], z, ic).wait_recv()
+    for made in z_copies + sent:
+        made.wait_send()
+
+
+def gather(n, m, tokens, out_grad):
+    rows, cols = tokens.shape
+    vmem = pl.BlockSpec(memory_space=pltpu.VMEM)
+    return pl.pallas_call(
+        functools.partial(gather_kernel, n),
+        out_shape=(
+            jax.ShapeDtypeStruct((n, rows, m * cols), BF),
+            jax.ShapeDtypeStruct((3, rows, m * cols), BF),
+        ),
+        in_specs=[vmem, vmem],
+        out_specs=(vmem, vmem),
+        scratch_shapes=[
+            pltpu.SemaphoreType.DMA((n + 1,)),
+            pltpu.SemaphoreType.DMA((n + 3, 3)),
+            pltpu.SemaphoreType.DMA((n + 3, 4)),
+        ],
+        compiler_params=pltpu.CompilerParams(
+            collective_id=0, has_side_effects=True, vmem_limit_bytes=32 * 1024 * 1024
+        ),
+    )(tokens, out_grad)
+
+
+def scatter_kernel(
+    n, h_ref, w_ref, out_ref, own, oth, a_out, a_in, b_out, b_in, c_out, c_in, send, recv
+):
+    z, i, ix, ic, ixc = places()
+    x = i // 2
+    cols = out_ref.shape[1]
+    order = [k for k in range(2, n - 1)] + [1, n - 1, 0]
+
+    def copy(src, dst, stage, k, blk, inner):
+        return pltpu.make_async_remote_copy(
+            src_ref=src, dst_ref=dst, send_sem=send.at[stage, k], recv_sem=recv.at[stage, k],
+            device_id={"blk": blk, "inner": inner}, device_id_type=MESH,
+        )
+
+    greet(z, i, n, ix, ic)
+
+    def share(k, inner):
+        return jnp.dot(
+            h_ref[lax.rem(z + k, n)],
+            w_ref[:, pl.ds(pl.multiple_of(inner * cols, cols), cols)],
+            preferred_element_type=F32,
+        )
+
+    sent = []
+
+    def go(made):
+        made.start()
+        sent.append(made)
+
+    for k in order:
+        a_out[k, 0] = share(k, ixc).astype(BF)
+        a_out[k, 1] = share(k, ic).astype(BF)
+        go(copy(a_out.at[k], a_in.at[k], 0, k, z, ic))
+        oth[k] = share(k, ix)
+        own[k] = share(k, i)
+    for k in order:
+        copy(a_out.at[k], a_in.at[k], 0, k, z, ic).wait_recv()
+        b_out[k] = (oth[k] + a_in[k, 0].astype(F32)).astype(BF)
+        go(copy(b_out.at[k], b_in.at[k], 1, k, z, ix))
+    for k in order:
+        copy(b_out.at[k], b_in.at[k], 1, k, z, ix).wait_recv()
+        total = own[k] + a_in[k, 1].astype(F32) + b_in[k].astype(F32)
+        if k:
+            c_out[k] = total.astype(BF)
+            go(copy(c_out.at[k], c_in.at[k], 2, k, lax.rem(z + k, n), i))
+    for k in range(1, n):
+        copy(c_out.at[k], c_in.at[k], 2, k, lax.rem(z + k, n), i).wait_recv()
+        total = total + c_in[k].astype(F32)
+    out_ref[...] = total.astype(BF)
+    for made in sent:
+        made.wait_send()
+
+
+def scatter(n, m, hidden, w_down):
+    _, rows, _ = hidden.shape
+    cols = w_down.shape[1] // m
+    vmem = pl.BlockSpec(memory_space=pltpu.VMEM)
+    return pl.pallas_call(
+        functools.partial(scatter_kernel, n),
+        out_shape=jax.ShapeDtypeStruct((rows, cols), BF),
+        in_specs=[vmem, vmem],
+        out_specs=vmem,
+        scratch_shapes=[
+            pltpu.VMEM((n, rows, cols), F32),
+            pltpu.VMEM((n, rows, cols), F32),
+            pltpu.VMEM((n, 2, rows, cols), BF),
+            pltpu.VMEM((n, 2, rows, cols), BF),
+            pltpu.VMEM((n, rows, cols), BF),
+            pltpu.VMEM((n, rows, cols), BF),
+            pltpu.VMEM((n, rows, cols), BF),
+            pltpu.VMEM((n, rows, cols), BF),
+            pltpu.SemaphoreType.DMA((3, n)),
+            pltpu.SemaphoreType.DMA((3, n)),
+        ],
+        compiler_params=pltpu.CompilerParams(
+            collective_id=1, has_side_effects=True, vmem_limit_bytes=32 * 1024 * 1024
+        ),
+    )(hidden, w_down)
+
+
+def on_square(tokens, out_grad, w_gate, w_up, w_down):
+    n, m = lax.axis_size("blk"), lax.axis_size("inner")
+    b = lax.axis_index("blk")
+    rows = tokens.shape[0]
+    units, width = w_gate.shape
+
+    x, y = gather(n, m, tokens, out_grad)
+
+    def pair(array, first):
+        return jnp.concatenate(
+            [lax.dynamic_index_in_dim(array, (first + j) % n, 0, keepdims=False) for j in (0, 1)], 0
+        )
+
+    flat = x.reshape(n * rows, width)
+    gate = nt(flat, w_gate)
+    up = nt(flat, w_up)
+    hidden = (jax.nn.silu(gate) * up).astype(BF).reshape(n, rows, units)
+
+    gate_2 = pair(gate.reshape(n, rows, units), b)
+    up_2 = pair(up.reshape(n, rows, units), b)
+    hidden_2 = pair(hidden, b)
+    back = nt(y[1:].reshape(2 * rows, width), w_down)
+    sigma = jax.nn.sigmoid(gate_2)
+    dgate = (back * up_2 * sigma * (1.0 + gate_2 * (1.0 - sigma))).astype(BF)
+    dup = (back * gate_2 * sigma).astype(BF)
+    moved = [shifted(part, "blk", 1) for part in (hidden_2, dgate, dup)]
+    mixed = scatter(n, m, hidden, w_down)
+
+    x_2 = pair(x, b - 1 + n)
+    y_2 = y[:2].reshape(2 * rows, width)
+    return (mixed, tn(moved[1], x_2), tn(moved[2], x_2), tn(moved[0], y_2))
+
+
 def solution(mesh):
+    square = mesh.shape["inner"] == 4 and mesh.shape["blk"] == 4
     return jax.shard_map(
-        on_device,
+        on_square if square else on_device,
         mesh=mesh,
         in_specs=(
             P(("groups", "blk"), "inner"),

time: 157 us -> 119 us (0.76)
  the two profiles are of different devices: /device:TPU:0 before, /device:TPU:17 now
where the time goes in v2:
time: 119 us
  Pallas kernels  76.9 us (65%)
  matrix products  20.7 us (17%)
  local copies, waits for them, and re-layouts  10.1 us (8%)
  starting transfers between devices  9.56 us (8%)
    pallas_call x1, Pallas kernels, gather(): pl.pallas_call(functools.partial(gather_kernel, n), out_shape=(jax.ShapeD...  38.5 us
    pallas_call x1, Pallas kernels, scatter(): pl.pallas_call(functools.partial(scatter_kernel, n), out_shape=jax.ShapeD...  38.4 us
    dot_general x3, matrix products, tn(): lax.dot_general(a, b, (((0,), (0,)), ((), ())), preferred_element_type=F32)  12 us
    ppermute x3, starting transfers between devices, shifted(): lax.ppermute(array, axis, [(i, (i + by) % count) for i in range(count)])  9.56 us
    dot_general x3, matrix products, nt(): lax.dot_general(a, b, (((1,), (1,)), ((), ())), preferred_element_type=F32)  8.68 us
    unnamed x19, local copies, waits for them, and re-layouts  6.15 us
  transfers between devices with their start and end apart: 3, of which 0 were waited for; matrix products, arithmetic and copies ran while one was open for 9% of the time, Pallas kernels for 32%

profile of v2, /device:TPU:17, one launch (start us, length us, event | category | flops | bytes accessed | tf_op | source)
XLA Modules:
  0.0 118.9 jit_solution(1531053905344322367)
XLA Ops:
  0.6 0.0 copy-start
  0.7 1.1 copy-done.5
  1.7 0.9 copy-done.6
  2.7 38.5 %shard_map.84 = (bf16[4,192,2048]{2,1,0:T(8,128)(2,1)S(1)}, bf16[3,192,2048]{2,1,0:T(8,128)(2,1)S(1)}) custom-call(bf16[192,512]{1,0:T(8,128)(2,1)S(1)} %copy-done.5, bf16[192,512]{1,0:T(8,128)(2,1)S(1)} %copy-done.6), custom_call_target="tpu_custom_call" | custom-call | tf_op jit(solution)/shard_map/pallas_call | solution.py:173
  41.2 0.0 copy-start.3
  41.2 1.7 %copy-done.3 = bf16[4,192,2048]{2,1,0:T(8,128)(2,1)} copy-done((bf16[4,192,2048]{2,1,0:T(8,128)(2,1)}, bf16[4,192,2048]{2,1,0:T(8,128)(2,1)S(1)}, u32[]{:S(2)}) %copy-start.3) | copy-done | bytes 3145752
  42.9 2.1 %fusion.7 = (bf16[2,192,2048]{2,1,0:T(8,128)(2,1)}, bf16[2,192,2048]{2,1,0:T(8,128)(2,1)}) fusion(bf16[3,192,2048]{2,1,0:T(8,128)(2,1)S(1)} %get-tuple-element.7), kind=kLoop, calls=%fused_computation.22 | loop fusion | bytes 6291456 | tf_op jit(solution)/shard_map/slice | solution.py:301
  45.0 4.5 %fusion.8 = f32[768,512]{1,0:T(8,128)S(1)} fusion(bf16[768,2048]{1,0:T(8,128)(2,1)} %bitcast.34, bf16[512,2048]{1,0:T(8,128)(2,1)} %param.7), kind=kOutput, calls=%fused_computation.23 | convolution fusion | flops 1610612736 | bytes 6815744 | tf_op jit(solution)/shard_map/dot_general | solution.py:20
  49.6 0.0 copy-start.8
  49.6 2.1 %multiply_convert_fusion = (bf16[768,512]{1,0:T(8,128)(2,1)S(1)}, f32[768,512]{1,0:T(8,128)S(1)}) fusion(f32[768,512]{1,0:T(8,128)S(1)} %fusion.8, bf16[768,2048]{1,0:T(8,128)(2,1)S(1)} %bitcast.35, bf16[512,2048]{1,0:T(8,128)(2,1)S(1)} %copy-done), kind=kOutput, calls=%fused_computation.1 | convolution fusion | flops 1612972032 | bytes 9175040 | tf_op jit(solution)/shard_map/dot_general | solution.py:20
  51.7 0.1 dynamic-slice_bitcast_fusion.3
  51.8 1.4 %copy-done.1 = bf16[512,2048]{1,0:T(8,128)(2,1)S(1)} copy-done((bf16[512,2048]{1,0:T(8,128)(2,1)S(1)}, bf16[512,2048]{1,0:T(8,128)(2,1)}, u32[]{:S(2)}) %copy-start.1) | copy-done | bytes 2097176
  53.2 2.1 %multiply_convert_fusion.1 = (bf16[384,512]{1,0:T(8,128)(2,1)}, bf16[384,512]{1,0:T(8,128)(2,1)}) fusion(f32[192,512]{1,0:T(8,128)S(1)} %get-tuple-element.15, f32[192,512]{1,0:T(8,128)S(1)} %get-tuple-element.14, f32[192,512]{1,0:T(8,128)S(1)} %get-tuple-element.22, f32[192,512]{1,0:T(8,128)S(1)} %get-tuple-element.23, bf16[384,2048]{1,0:T(8,128)(2,1)S(1)} %bitcast.37, ...), kind=kOutput, calls=%fused_computation.9 | convolution fusion | flops 808255488 | bytes 6029312 | tf_op jit(solution)/shard_map/dot_general | solution.py:20
  55.4 0.7 collective-permute-start
  56.1 0.8 pad_maximum_fusion.4
  56.9 0.1 collective-permute-start.2
  57.0 8.8 %collective-permute-start.1 = (bf16[384,512]{1,0:T(8,128)(2,1)}, bf16[384,512]{1,0:T(8,128)(2,1)}, u32[]{:S(2)}, u32[]{:S(2)}) collective-permute-start(bf16[384,512]{1,0:T(8,128)(2,1)} %get-tuple-element.12), channel_id=1, source_target_pairs={{0,4},{4,8},{8,12},{12,0},{1,5},{5,9},{9,13},{13,1},{2,6},{6,10},{... | collective-permute-start | bytes 1179656 | tf_op jit(solution)/shard_map/ppermute | solution.py:16
  65.7 1.7 %dynamic-slice_bitcast_fusion.1 = (bf16[192,2048]{1,0:T(8,128)(2,1)S(1)}, bf16[192,2048]{1,0:T(8,128)(2,1)S(1)}) fusion(bf16[4,192,2048]{2,1,0:T(8,128)(2,1)} %copy-done.3, s32[]{:T(128)S(6)} %select_n.51, s32[]{:T(128)S(6)} %select_n.53), kind=kLoop, calls=%fused_computation.11 | loop fusion | bytes 3145736 | tf_op jit(solution)/shard_map/jit(dynamic_index_in_dim)/squeeze | solution.py:282
  67.4 0.4 copy-done.2
  67.8 38.4 %shard_map.85 = bf16[192,512]{1,0:T(8,128)(2,1)S(1)} custom-call(bf16[4,192,512]{2,1,0:T(8,128)(2,1)S(1)} %bitcast.33, bf16[512,2048]{1,0:T(8,128)(2,1)S(1)} %copy-done.2), custom_call_target="tpu_custom_call" | custom-call | tf_op jit(solution)/shard_map/pallas_call | solution.py:249
  106.2 4.3 %fusion.1 = f32[512,2048]{1,0:T(8,128)} fusion(bf16[384,512]{1,0:T(8,128)(2,1)} %collective-permute-done, bf16[192,2048]{1,0:T(8,128)(2,1)S(1)} %get-tuple-element.9, bf16[192,2048]{1,0:T(8,128)(2,1)S(1)} %get-tuple-element.8), kind=kOutput, calls=%fused_computation.3 | convolution fusion | flops 808452096 | bytes 6160384 | tf_op jit(solution)/shard_map/dot_general | solution.py:24
  110.5 4.4 %fusion = f32[512,2048]{1,0:T(8,128)} fusion(bf16[384,512]{1,0:T(8,128)(2,1)} %collective-permute-done.1, bf16[192,2048]{1,0:T(8,128)(2,1)S(1)} %get-tuple-element.9, bf16[192,2048]{1,0:T(8,128)(2,1)S(1)} %get-tuple-element.8), kind=kOutput, calls=%fused_computation.2 | convolution fusion | flops 808452096 | bytes 6160384 | tf_op jit(solution)/shard_map/dot_general | solution.py:24
  114.9 3.3 %fusion.9 = f32[512,2048]{1,0:T(8,128)} fusion(bf16[384,512]{1,0:T(8,128)(2,1)S(1)} %collective-permute-done.2, bf16[384,2048]{1,0:T(8,128)(2,1)S(1)} %bitcast.36), kind=kOutput, calls=%fused_computation.24 | convolution fusion | flops 805306368 | bytes 6160384 | tf_op jit(solution)/shard_map/dot_general | solution.py:24
  118.3 0.7 copy.10
  (14 shorter events, 0.1 us)
Async XLA Ops:
  0.6 48.9 %copy-start = (bf16[512,2048]{1,0:T(8,128)(2,1)S(1)}, bf16[512,2048]{1,0:T(8,128)(2,1)}, u32[]{:S(2)}) copy-start(bf16[512,2048]{1,0:T(8,128)(2,1)} %param.8) | copy-start | bytes 6291460
  0.7 1.1 copy-start.5
  1.7 0.9 copy-start.6
  41.2 1.7 %copy-start.3 = (bf16[4,192,2048]{2,1,0:T(8,128)(2,1)}, bf16[4,192,2048]{2,1,0:T(8,128)(2,1)S(1)}, u32[]{:S(2)}) copy-start(bf16[4,192,2048]{2,1,0:T(8,128)(2,1)S(1)} %get-tuple-element.6) | copy-start | bytes 9437188
  45.0 4.5 %copy-start.4 = (bf16[4,192,2048]{2,1,0:T(8,128)(2,1)S(1)}, bf16[4,192,2048]{2,1,0:T(8,128)(2,1)}, u32[]{:S(2)}) copy-start(bf16[4,192,2048]{2,1,0:T(8,128)(2,1)} %copy-done.3) | copy-start | bytes 9437188
  49.6 2.2 %copy-start.8 = (bf16[2,192,2048]{2,1,0:T(8,128)(2,1)S(1)}, bf16[2,192,2048]{2,1,0:T(8,128)(2,1)}, u32[]{:S(2)}) copy-start(bf16[2,192,2048]{2,1,0:T(8,128)(2,1)} %get-tuple-element.11) | copy-start | bytes 4718596
  51.7 1.6 %copy-start.1 = (bf16[512,2048]{1,0:T(8,128)(2,1)S(1)}, bf16[512,2048]{1,0:T(8,128)(2,1)}, u32[]{:S(2)}) copy-start(bf16[512,2048]{1,0:T(8,128)(2,1)} %w_ref.1) | copy-start | bytes 6291460
  55.4 50.9 %collective-permute-start = (bf16[384,512]{1,0:T(8,128)(2,1)}, bf16[384,512]{1,0:T(8,128)(2,1)}, u32[]{:S(2)}, u32[]{:S(2)}) collective-permute-start(bf16[384,512]{1,0:T(8,128)(2,1)} %get-tuple-element.13), channel_id=1, source_target_pairs={{0,4},{4,8},{8,12},{12,0},{1,5},{5,9},{9,13},{13,1},{2,6},{6,10},{... | collective-permute-start | bytes 1179656 | tf_op jit(solution)/shard_map/ppermute | solution.py:16
  56.9 58.0 %collective-permute-start.2 = (bf16[384,512]{1,0:T(8,128)(2,1)}, bf16[384,512]{1,0:T(8,128)(2,1)S(1)}, u32[]{:S(2)}, u32[]{:S(2)}) collective-permute-start(bf16[384,512]{1,0:T(8,128)(2,1)} %pad_maximum_fusion.4), channel_id=1, source_target_pairs={{0,4},{4,8},{8,12},{12,0},{1,5},{5,9},{9,13},{13,1},{2,6},{6,10},{... | collective-permute-start | bytes 1179656 | tf_op jit(solution)/shard_map/ppermute | solution.py:16
  57.0 53.5 %collective-permute-start.1 = (bf16[384,512]{1,0:T(8,128)(2,1)}, bf16[384,512]{1,0:T(8,128)(2,1)}, u32[]{:S(2)}, u32[]{:S(2)}) collective-permute-start(bf16[384,512]{1,0:T(8,128)(2,1)} %get-tuple-element.12), channel_id=1, source_target_pairs={{0,4},{4,8},{8,12},{12,0},{1,5},{5,9},{9,13},{13,1},{2,6},{6,10},{... | collective-permute-start | bytes 1179656 | tf_op jit(solution)/shard_map/ppermute | solution.py:16
  65.7 2.1 %copy-start.2 = (bf16[512,2048]{1,0:T(8,128)(2,1)S(1)}, bf16[512,2048]{1,0:T(8,128)(2,1)}, u32[]{:S(2)}) copy-start(bf16[512,2048]{1,0:T(8,128)(2,1)} %w_ref.1) | copy-start | bytes 6291460
  110.5 4.4 %copy-start.7 = (bf16[2,192,2048]{2,1,0:T(8,128)(2,1)S(1)}, bf16[2,192,2048]{2,1,0:T(8,128)(2,1)}, u32[]{:S(2)}) copy-start(bf16[2,192,2048]{2,1,0:T(8,128)(2,1)} %get-tuple-element.10) | copy-start | bytes 4718596

commit v3 on v1

--- a/solution.py
+++ b/solution.py
@@ -1,6 +1,10 @@
+import functools
+
 import jax
 import jax.numpy as jnp
 from jax import lax
+from jax.experimental import pallas as pl
+from jax.experimental.pallas import tpu as pltpu
 from jax.sharding import PartitionSpec as P
 
 BF = jnp.bfloat16
@@ -61,9 +65,261 @@
     return (mixed, tn(moved[0], x_2), tn(moved[1], x_2), tn(moved[2], y_2))
 
 
+MESH = pl.DeviceIdType.MESH
+
+
+def remote(src, dst, ssem, rsem, blk, inner):
+    return pltpu.make_async_remote_copy(
+        src_ref=src, dst_ref=dst, send_sem=ssem, recv_sem=rsem,
+        device_id={"blk": blk, "inner": inner}, device_id_type=MESH,
+    )
+
+
+def greet(z, i, n, ix, ic):
+    barrier = pltpu.get_barrier_semaphore()
+    for k in range(1, n):
+        pl.semaphore_signal(
+            barrier, inc=1, device_id={"blk": lax.rem(z + k, n), "inner": i}, device_id_type=MESH
+        )
+    for other in (ix, ic):
+        pl.semaphore_signal(
+            barrier, inc=1, device_id={"blk": z, "inner": other}, device_id_type=MESH
+        )
+    pl.semaphore_wait(barrier, n + 1)
+
+
+def step_kernel(
+    n, t_ref, g_ref, wg_hbm, wu_hbm, wd_hbm,
+    x_out, y_out, m_in, c_out, own_out,
+    x_rest, y_next, wg, wu, wd, hid, m_out, own, oth, a_out, a_in, b_out, b_in,
+    local, zsend, send, recv, msend, mrecv, rsend, rrecv,
+):
+    z, i = lax.axis_index("blk"), lax.axis_index("inner")
+    x, c = i // 2, lax.rem(i, 2)
+    ix, ic, ixc = (1 - x) * 2 + c, x * 2 + (1 - c), (1 - x) * 2 + (1 - c)
+    rows, cols = t_ref.shape
+    units = hid.shape[2]
+
+    def part(inner):
+        return pl.ds(pl.multiple_of(inner * cols, cols), cols)
+
+    def block(q):
+        if q < n:
+            return x_out.at[q] if q < 2 else x_rest.at[q - 2]
+        return y_out.at[q - n] if q < n + 2 else y_next.at[0]
+
+    def view(q, inner):
+        return block(q).at[:, part(inner)]
+
+    loads = [
+        pltpu.make_async_copy(wg_hbm, wg, local.at[0]),
+        pltpu.make_async_copy(wu_hbm, wu, local.at[1]),
+        pltpu.make_async_copy(wd_hbm, wd, local.at[2]),
+        pltpu.make_async_copy(t_ref, view(1, i), local.at[3]),
+        pltpu.make_async_copy(g_ref, view(n + 1, i), local.at[4]),
+    ]
+    for load in (loads[3], loads[4], loads[0], loads[1], loads[2]):
+        load.start()
+    greet(z, i, n, ix, ic)
+
+    sent = []
+
+    def go(made):
+        made.start()
+        sent.append(made)
+
+    def first(q):
+        src = view(q, i)
+        if q == 1:
+            src = t_ref
+        elif q == n + 1:
+            src = g_ref
+        else:
+            remote(src, src, send.at[q, 0], recv.at[q, 0], z, ix).wait_recv()
+        go(remote(src, view(q, i), send.at[q, 0], recv.at[q, 1], z, ix))
+        go(remote(src, view(q, i), send.at[q, 1], recv.at[q, 2], z, ic))
+
+    def second(q):
+        v = view(q, ix)
+        remote(v, v, send.at[q, 1], recv.at[q, 1], z, ix).wait_recv()
+        go(remote(v, v, send.at[q, 2], recv.at[q, 3], z, ic))
+
+    def whole(q):
+        for inner, sem in ((ic, 2), (ixc, 3)):
+            v = view(q, inner)
+            remote(v, v, send.at[q, 1], recv.at[q, sem], z, ic).wait_recv()
+
+    def z_send(src, q, k, at):
+        go(remote(src, view(q, i), zsend.at[at], recv.at[q, 0], lax.rem(z + k, n), i))
+
+    def forward(s):
+        half = units // 2
+        for u in range(2):
+            span = pl.ds(u * half, half)
+            rows_x = block(s)[...]
+            gate = nt(rows_x, wg[span, :])
+            up = nt(rows_x, wu[span, :])
+            sigma = jax.nn.sigmoid(gate)
+            active = gate * sigma
+            hidden = (active * up).astype(BF)
+            hid[s, :, span] = hidden
+            if s in (1, 2):
+                back = nt(block(n + s)[...], wd[span, :])
+                m_out[s - 1, 0, :, span] = (
+                    back * up * sigma * (1.0 + gate * (1.0 - sigma))
+                ).astype(BF)
+                m_out[s - 1, 1, :, span] = (back * active).astype(BF)
+                m_out[s - 1, 2, :, span] = hidden
+        if s in (1, 2):
+            go(m_copy(s - 1))
+
+    def m_copy(j):
+        return remote(
+            m_out.at[j], m_in.at[:, pl.ds(j * rows, rows), :],
+            msend.at[j], mrecv.at[j], lax.rem(z + 1, n), i,
+        )
+
+    def share(s, inner):
+        return jnp.dot(hid[s], wd[:, part(inner)], preferred_element_type=F32)
+
+    def a_copy(s):
+        return remote(a_out.at[s], a_in.at[s], rsend.at[0, s], rrecv.at[0, s], z, ic)
+
+    def b_copy(s):
+        return remote(b_out.at[s], b_in.at[s], rsend.at[1, s], rrecv.at[1, s], z, ix)
+
+    def stage_a(s):
+        a_out[s, 0] = share(s, ixc).astype(BF)
+        a_out[s, 1] = share(s, ic).astype(BF)
+        go(a_copy(s))
+        oth[s] = share(s, ix)
+        own[s] = share(s, i)
+
+    def stage_b(s):
+        a_copy(s).wait_recv()
+        b_out[s] = (oth[s] + a_in[s, 0].astype(F32)).astype(BF)
+        go(b_copy(s))
+
+    def stage_c(s):
+        b_copy(s).wait_recv()
+        total = own[s] + a_in[s, 1].astype(F32) + b_in[s].astype(F32)
+        if s == 1:
+            own_out[...] = total
+        else:
+            c_out[s if s == 0 else s - 1] = total.astype(BF)
+
+    first(1)
+    first(n + 1)
+    z_send(t_ref, 0, 1, 0)
+    z_send(t_ref, 2, n - 1, 1)
+    z_send(g_ref, n + 2, n - 1, 2)
+    for k in range(2, n - 1):
+        z_send(t_ref, n - k + 1, k, 2 + k)
+    z_send(g_ref, n, 1, 3)
+    second(1)
+    second(n + 1)
+    first(2)
+    first(n + 2)
+    for load in loads:
+        load.wait()
+    whole(1)
+    whole(n + 1)
+    forward(1)
+    first(0)
+    second(2)
+    second(n + 2)
+    stage_a(1)
+    whole(2)
+    whole(n + 2)
+    forward(2)
+    for s in range(3, n):
+        first(s)
+    second(0)
+    stage_a(2)
+    stage_b(2)
+    whole(0)
+    forward(0)
+    for s in range(3, n):
+        second(s)
+    stage_a(0)
+    stage_b(0)
+    first(n)
+    for s in range(3, n):
+        whole(s)
+        forward(s)
+        stage_a(s)
+        stage_b(s)
+    stage_b(1)
+    second(n)
+    stage_c(2)
+    stage_c(0)
+    for s in range(3, n):
+        stage_c(s)
+    stage_c(1)
+    whole(n)
+    for j in range(2):
+        m_copy(j).wait_recv()
+    for made in sent:
+        made.wait_send()
+
+
+def on_square(tokens, out_grad, w_gate, w_up, w_down):
+    n, m = lax.axis_size("blk"), lax.axis_size("inner")
+    rows, cols = tokens.shape
+    units, width = w_gate.shape
+    vmem = pl.BlockSpec(memory_space=pltpu.VMEM)
+    hbm = pl.BlockSpec(memory_space=pl.ANY)
+    dma = pltpu.SemaphoreType.DMA
+    x, y, moved, parts, total = pl.pallas_call(
+        functools.partial(step_kernel, n),
+        out_shape=(
+            jax.ShapeDtypeStruct((2, rows, width), BF),
+            jax.ShapeDtypeStruct((2, rows, width), BF),
+            jax.ShapeDtypeStruct((3, 2 * rows, units), BF),
+            jax.ShapeDtypeStruct((n - 1, rows, cols), BF),
+            jax.ShapeDtypeStruct((rows, cols), F32),
+        ),
+        in_specs=[hbm] * 5,
+        out_specs=(vmem,) * 5,
+        scratch_shapes=[
+            pltpu.VMEM((n - 2, rows, width), BF),
+            pltpu.VMEM((1, rows, width), BF),
+            pltpu.VMEM((units, width), BF),
+            pltpu.VMEM((units, width), BF),
+            pltpu.VMEM((units, width), BF),
+            pltpu.VMEM((n, rows, units), BF),
+            pltpu.VMEM((2, 3, rows, units), BF),
+            pltpu.VMEM((n, rows, cols), F32),
+            pltpu.VMEM((n, rows, cols), F32),
+            pltpu.VMEM((n, 2, rows, cols), BF),
+            pltpu.VMEM((n, 2, rows, cols), BF),
+            pltpu.VMEM((n, rows, cols), BF),
+            pltpu.VMEM((n, rows, cols), BF),
+            dma((5,)),
+            dma((n + 1,)),
+            dma((n + 3, 3)),
+            dma((n + 3, 4)),
+            dma((2,)),
+            dma((2,)),
+            dma((2, n)),
+            dma((2, n)),
+        ],
+        compiler_params=pltpu.CompilerParams(
+            collective_id=0, has_side_effects=True, vmem_limit_bytes=56 * 1024 * 1024
+        ),
+    )(tokens, out_grad, w_gate, w_up, w_down)
+
+    for at, by in enumerate([-1] + list(range(1, n - 1))):
+        total = total + shifted(parts[at], "blk", by).astype(F32)
+    x_2 = x.reshape(2 * rows, width)
+    y_2 = y.reshape(2 * rows, width)
+    return (total.astype(BF), tn(moved[0], x_2), tn(moved[1], x_2), tn(moved[2], y_2))
+
+
 def solution(mesh):
+    square = mesh.shape["inner"] == 4 and mesh.shape["blk"] == 4
     return jax.shard_map(
-        on_device,
+        on_square if square else on_device,
         mesh=mesh,
         in_specs=(
             P(("groups", "blk"), "inner"),

time: 157 us -> 107 us (0.68)
  Pallas kernels: 0 us -> 87.3 us
  waiting for transfers between devices: 86 us -> 2.51 us
  blocking collectives: 21.9 us -> 0 us
  between operations: 13.9 us -> 0.67 us
  matrix products: 23.8 us -> 11.6 us
  starting transfers between devices: 5.52 us -> 2.07 us
  local copies, waits for them, and re-layouts: 4.03 us -> 1.17 us
    pallas_call x0 -> x1, Pallas kernels: none -> 87.3 us  [on_square(): pl.pallas_call(functools.partial(step_kernel, n), out_shape=(jax.ShapeDty...]
    reduce_scatter x2 -> x0, waiting for transfers between devices: 50.4 us -> none  [the longest x1 35.7 us: on_device(): mixed = lax.psum_scatter(partial, 'inner', scatter_dimension=1, tiled=True)]
    all_gather x2 -> x0, waiting for transfers between devices: 30.9 us -> none  [the longest x1 19 us: on_device(): x = lax.all_gather(x_cols, 'inner', axis=1, tiled=True)]
    all_gather x1 -> x0, blocking collectives: 21.9 us -> none  [on_device(): x_cols = lax.all_gather(tokens, 'blk', axis=0, tiled=True)]
    dot_general x4 -> x0, matrix products: 13.8 us -> none  [the longest x3 10.4 us: nt(): lax.dot_general(a, b, (((1,), (1,)), ((), ())), preferred_element_type=F32)]
    dynamic_slice x4 -> x0, local copies, waits for them, and re-layouts: 3.71 us -> none  [block(): return lax.dynamic_slice_in_dim(array, index % n * rows, rows, 0)]
    ppermute x3, starting transfers between devices: 5.36 us -> 2.07 us  [shifted(): lax.ppermute(array, axis, [(i, (i + by) % count) for i in range(count)])]
    ppermute x3, waiting for transfers between devices: 4.6 us -> 2.51 us  [shifted(): lax.ppermute(array, axis, [(i, (i + by) % count) for i in range(count)])]
  transfers between devices with their start and end apart: 7 -> 3, of which waited for: 6 -> 1; matrix products, arithmetic and copies ran while one was open for 19% -> 11% of each run, Pallas kernels for 0% -> 0%
where the time goes in v3:
time: 107 us; the launch traced here: 106 us
  Pallas kernels  87.3 us (82%)
  matrix products  11.6 us (11%)
  waiting for transfers between devices  2.51 us (2%)
  starting transfers between devices  2.07 us (2%)
  local copies, waits for them, and re-layouts  1.17 us (1%)
    pallas_call x1, Pallas kernels, on_square(): pl.pallas_call(functools.partial(step_kernel, n), out_shape=(jax.ShapeDty...  87.3 us
    dot_general x3, matrix products, tn(): lax.dot_general(a, b, (((0,), (0,)), ((), ())), preferred_element_type=F32)  11.6 us
    ppermute x3, waiting for transfers between devices, shifted(): lax.ppermute(array, axis, [(i, (i + by) % count) for i in range(count)])  2.51 us
  transfers between devices with their start and end apart: 3, of which 1 were waited for; matrix products, arithmetic and copies ran while one was open for 11% of the time, Pallas kernels for 0%

profile of v3, /device:TPU:0, one launch (start us, length us, event | category | flops | bytes accessed | tf_op | source)
XLA Modules:
  0.0 106.1 jit_solution(13428541585118941254)
XLA Ops:
  0.6 87.3 %shard_map.84 = (bf16[2,192,2048]{2,1,0:T(8,128)(2,1)}, bf16[2,192,2048]{2,1,0:T(8,128)(2,1)}, bf16[3,384,512]{2,1,0:T(8,128)(2,1)}, bf16[3,192,512]{2,1,0:T(8,128)(2,1)}, f32[192,512]{1,0:T(8,128)}) custom-call(bf16[192,512]{1,0:T(8,128)(2,1)} %t_ref.1, bf16[192,512]{1,0:T(8,128)(2,1)} %g_ref.1, bf16[512,2048]{1,0:T(8,128)(2,1)} %wg_hbm.1, ...), custom_call_target="tpu_custom_call" | custom-call | tf_op jit(solution)/shard_map/pallas_call | solution.py:273
  88.0 1.2 %slice_bitcast_fusion.2 = (bf16[192,512]{1,0:T(8,128)(2,1)S(1)}, bf16[192,512]{1,0:T(8,128)(2,1)S(1)}, bf16[192,512]{1,0:T(8,128)(2,1)S(1)}) fusion(bf16[3,192,512]{2,1,0:T(8,128)(2,1)} %get-tuple-element.10), kind=kLoop, calls=%fused_computation.12 | loop fusion | bytes 1179648 | tf_op jit(solution)/shard_map/squeeze | solution.py:313
  89.1 0.1 collective-permute-start
  89.2 0.1 collective-permute-start.2
  89.3 1.9 %collective-permute-start.1 = (bf16[192,512]{1,0:T(8,128)(2,1)S(1)}, bf16[192,512]{1,0:T(8,128)(2,1)S(1)}, u32[]{:S(2)}, u32[]{:S(2)}) collective-permute-start(bf16[192,512]{1,0:T(8,128)(2,1)S(1)} %get-tuple-element.16), channel_id=1, source_target_pairs={{0,4},{4,8},{8,12},{12,0},{1,5},{5,9},{9,13},{13,1},{2,6},{6,10},{... | collective-permute-start | bytes 589832 | tf_op jit(solution)/shard_map/ppermute | solution.py:16
  91.2 0.0 copy-start
  91.2 0.0 copy-start.2
  91.2 5.0 %fusion.2 = f32[512,2048]{1,0:T(8,128)} fusion(bf16[384,2048]{1,0:T(8,128)(2,1)} %bitcast.20, bf16[3,384,512]{2,1,0:T(8,128)(2,1)} %get-tuple-element.11), kind=kOutput, calls=%fused_computation.2 | convolution fusion | flops 805306368 | bytes 6160384 | tf_op jit(solution)/shard_map/dot_general | solution.py:24
  96.2 0.0 copy-done
  96.2 0.0 copy-done.2
  96.2 0.0 copy-start.1
  96.2 3.3 %fusion.4 = f32[512,2048]{1,0:T(8,128)} fusion(bf16[384,2048]{1,0:T(8,128)(2,1)S(1)} %bitcast.21, bf16[3,384,512]{2,1,0:T(8,128)(2,1)S(1)} %copy-done.2), kind=kOutput, calls=%fused_computation.4 | convolution fusion | flops 805306368 | bytes 6160384 | tf_op jit(solution)/shard_map/dot_general | solution.py:24
  99.5 0.0 copy-done.1
  99.5 0.0 copy-start.3
  99.5 3.3 %fusion = f32[512,2048]{1,0:T(8,128)} fusion(bf16[384,2048]{1,0:T(8,128)(2,1)S(1)} %bitcast.22, bf16[3,384,512]{2,1,0:T(8,128)(2,1)S(1)} %copy-done.2), kind=kOutput, calls=%fused_computation | convolution fusion | flops 805306368 | bytes 6160384 | tf_op jit(solution)/shard_map/dot_general | solution.py:24
  102.8 0.0 collective-permute-done
  102.8 2.5 %collective-permute-done.2 = bf16[192,512]{1,0:T(8,128)(2,1)S(1)} collective-permute-done((bf16[192,512]{1,0:T(8,128)(2,1)S(1)}, bf16[192,512]{1,0:T(8,128)(2,1)S(1)}, u32[]{:S(2)}, u32[]{:S(2)}) %collective-permute-start.2) | collective-permute-done | bytes 196640 | tf_op jit(solution)/shard_map/ppermute | solution.py:16
  105.3 0.0 collective-permute-done.1
  105.3 0.0 copy-done.3
  105.3 0.8 add_convert_fusion
Async XLA Ops:
  89.1 13.7 %collective-permute-start = (bf16[192,512]{1,0:T(8,128)(2,1)S(1)}, bf16[192,512]{1,0:T(8,128)(2,1)S(1)}, u32[]{:S(2)}, u32[]{:S(2)}) collective-permute-start(bf16[192,512]{1,0:T(8,128)(2,1)S(1)} %get-tuple-element.14), channel_id=1, source_target_pairs={{0,12},{4,0},{8,4},{12,8},{1,13},{5,1},{9,5},{13,9},{2,14},{6,2},{... | collective-permute-start | bytes 589832 | tf_op jit(solution)/shard_map/ppermute | solution.py:16
  89.2 16.1 %collective-permute-start.2 = (bf16[192,512]{1,0:T(8,128)(2,1)S(1)}, bf16[192,512]{1,0:T(8,128)(2,1)S(1)}, u32[]{:S(2)}, u32[]{:S(2)}) collective-permute-start(bf16[192,512]{1,0:T(8,128)(2,1)S(1)} %get-tuple-element.15), channel_id=1, source_target_pairs={{0,8},{4,12},{8,0},{12,4},{1,9},{5,13},{9,1},{13,5},{2,10},{6,14},... | collective-permute-start | bytes 589832 | tf_op jit(solution)/shard_map/ppermute | solution.py:16
  89.3 16.0 %collective-permute-start.1 = (bf16[192,512]{1,0:T(8,128)(2,1)S(1)}, bf16[192,512]{1,0:T(8,128)(2,1)S(1)}, u32[]{:S(2)}, u32[]{:S(2)}) collective-permute-start(bf16[192,512]{1,0:T(8,128)(2,1)S(1)} %get-tuple-element.16), channel_id=1, source_target_pairs={{0,4},{4,8},{8,12},{12,0},{1,5},{5,9},{9,13},{13,1},{2,6},{6,10},{... | collective-permute-start | bytes 589832 | tf_op jit(solution)/shard_map/ppermute | solution.py:16
  91.2 5.0 %copy-start = (bf16[2,192,2048]{2,1,0:T(8,128)(2,1)S(1)}, bf16[2,192,2048]{2,1,0:T(8,128)(2,1)}, u32[]{:S(2)}) copy-start(bf16[2,192,2048]{2,1,0:T(8,128)(2,1)} %get-tuple-element.12) | copy-start | bytes 4718596
  91.2 5.0 %copy-start.2 = (bf16[3,384,512]{2,1,0:T(8,128)(2,1)S(1)}, bf16[3,384,512]{2,1,0:T(8,128)(2,1)}, u32[]{:S(2)}) copy-start(bf16[3,384,512]{2,1,0:T(8,128)(2,1)} %get-tuple-element.11) | copy-start | bytes 3538948
  96.2 3.3 %copy-start.1 = (bf16[2,192,2048]{2,1,0:T(8,128)(2,1)S(1)}, bf16[2,192,2048]{2,1,0:T(8,128)(2,1)}, u32[]{:S(2)}) copy-start(bf16[2,192,2048]{2,1,0:T(8,128)(2,1)} %get-tuple-element.13) | copy-start | bytes 4718596
  99.5 5.8 %copy-start.3 = (f32[192,512]{1,0:T(8,128)S(1)}, f32[192,512]{1,0:T(8,128)}, u32[]{:S(2)}) copy-start(f32[192,512]{1,0:T(8,128)} %get-tuple-element.9) | copy-start | bytes 1179652

commit v4 on v3

--- a/solution.py
+++ b/solution.py
@@ -149,8 +149,8 @@
             v = view(q, inner)
             remote(v, v, send.at[q, 1], recv.at[q, sem], z, ic).wait_recv()
 
-    def z_send(src, q, k, at):
-        go(remote(src, view(q, i), zsend.at[at], recv.at[q, 0], lax.rem(z + k, n), i))
+    def z_copy(src, q, k, at):
+        return remote(src, view(q, i), zsend.at[at], recv.at[q, 0], lax.rem(z + k, n), i)
 
     def forward(s):
         half = units // 2
@@ -210,12 +210,26 @@
 
     first(1)
     first(n + 1)
-    z_send(t_ref, 0, 1, 0)
-    z_send(t_ref, 2, n - 1, 1)
-    z_send(g_ref, n + 2, n - 1, 2)
-    for k in range(2, n - 1):
-        z_send(t_ref, n - k + 1, k, 2 + k)
-    z_send(g_ref, n, 1, 3)
+    ups = [z_copy(t_ref, 0, 1, 0), z_copy(g_ref, n, 1, 3)]
+    downs = [z_copy(t_ref, 2, n - 1, 1), z_copy(g_ref, n + 2, n - 1, 2)]
+    fars = [z_copy(t_ref, n - k + 1, k, 2 + k) for k in range(2, n - 1)]
+
+    @pl.when(z == 0)
+    def _():
+        for made in ups + fars + downs:
+            made.start()
+
+    @pl.when(z == n - 1)
+    def _():
+        for made in downs + fars + ups:
+            made.start()
+
+    @pl.when((z > 0) & (z < n - 1))
+    def _():
+        for made in [ups[0]] + downs + fars + [ups[1]]:
+            made.start()
+
+    sent.extend(ups + downs + fars)
     second(1)
     second(n + 1)
     first(2)

time: 107 us -> 91.5 us (0.86)
  Pallas kernels: 87.3 us -> 61.2 us
  starting transfers between devices: 2.07 us -> 12.4 us
    pallas_call x1, Pallas kernels: 87.3 us -> 61.2 us  [on_square(): pl.pallas_call(functools.partial(step_kernel, n), out_shape=(jax.ShapeDty...]
    ppermute x3, starting transfers between devices: 2.07 us -> 12.4 us  [shifted(): lax.ppermute(array, axis, [(i, (i + by) % count) for i in range(count)])]
  transfers between devices with their start and end apart: 3 -> 3, of which waited for: 1 -> 1; matrix products, arithmetic and copies ran while one was open for 11% -> 13% of each run, Pallas kernels for 0% -> 0%
where the time goes in v4:
time: 91.5 us; the launch traced here: 91.3 us
  Pallas kernels  61.2 us (67%)
  starting transfers between devices  12.4 us (14%)
  matrix products  11.6 us (13%)
  waiting for transfers between devices  3.5 us (4%)
  local copies, waits for them, and re-layouts  1.17 us (1%)
    pallas_call x1, Pallas kernels, on_square(): pl.pallas_call(functools.partial(step_kernel, n), out_shape=(jax.ShapeDty...  61.2 us
    ppermute x3, starting transfers between devices, shifted(): lax.ppermute(array, axis, [(i, (i + by) % count) for i in range(count)])  12.4 us
    dot_general x3, matrix products, tn(): lax.dot_general(a, b, (((0,), (0,)), ((), ())), preferred_element_type=F32)  11.6 us
    ppermute x3, waiting for transfers between devices, shifted(): lax.ppermute(array, axis, [(i, (i + by) % count) for i in range(count)])  3.5 us
  transfers between devices with their start and end apart: 3, of which 1 were waited for; matrix products, arithmetic and copies ran while one was open for 13% of the time, Pallas kernels for 0%

profile of v4, /device:TPU:0, one launch (start us, length us, event | category | flops | bytes accessed | tf_op | source)
XLA Modules:
  0.0 91.3 jit_solution(7450558162446664289)
XLA Ops:
  0.6 61.2 %shard_map.84 = (bf16[2,192,2048]{2,1,0:T(8,128)(2,1)}, bf16[2,192,2048]{2,1,0:T(8,128)(2,1)}, bf16[3,384,512]{2,1,0:T(8,128)(2,1)}, bf16[3,192,512]{2,1,0:T(8,128)(2,1)}, f32[192,512]{1,0:T(8,128)}) custom-call(bf16[192,512]{1,0:T(8,128)(2,1)} %t_ref.1, bf16[192,512]{1,0:T(8,128)(2,1)} %g_ref.1, bf16[512,2048]{1,0:T(8,128)(2,1)} %wg_hbm.1, ...), custom_call_target="tpu_custom_call" | custom-call | tf_op jit(solution)/shard_map/pallas_call | solution.py:287
  61.9 1.2 %slice_bitcast_fusion.2 = (bf16[192,512]{1,0:T(8,128)(2,1)S(1)}, bf16[192,512]{1,0:T(8,128)(2,1)S(1)}, bf16[192,512]{1,0:T(8,128)(2,1)S(1)}) fusion(bf16[3,192,512]{2,1,0:T(8,128)(2,1)} %get-tuple-element.10), kind=kLoop, calls=%fused_computation.12 | loop fusion | bytes 1179648 | tf_op jit(solution)/shard_map/squeeze | solution.py:327
  63.0 11.8 %collective-permute-start = (bf16[192,512]{1,0:T(8,128)(2,1)S(1)}, bf16[192,512]{1,0:T(8,128)(2,1)S(1)}, u32[]{:S(2)}, u32[]{:S(2)}) collective-permute-start(bf16[192,512]{1,0:T(8,128)(2,1)S(1)} %get-tuple-element.14), channel_id=1, source_target_pairs={{0,12},{4,0},{8,4},{12,8},{1,13},{5,1},{9,5},{13,9},{2,14},{6,2},{... | collective-permute-start | bytes 589832 | tf_op jit(solution)/shard_map/ppermute | solution.py:16
  74.8 0.0 collective-permute-start.2
  74.8 0.6 collective-permute-start.1
  75.5 0.0 copy-start
  75.5 0.0 copy-start.2
  75.5 5.0 %fusion.2 = f32[512,2048]{1,0:T(8,128)} fusion(bf16[384,2048]{1,0:T(8,128)(2,1)} %bitcast.20, bf16[3,384,512]{2,1,0:T(8,128)(2,1)} %get-tuple-element.11), kind=kOutput, calls=%fused_computation.2 | convolution fusion | flops 805306368 | bytes 6160384 | tf_op jit(solution)/shard_map/dot_general | solution.py:24
  80.4 0.0 copy-done
  80.4 0.0 copy-done.2
  80.4 0.0 copy-start.1
  80.4 3.3 %fusion.4 = f32[512,2048]{1,0:T(8,128)} fusion(bf16[384,2048]{1,0:T(8,128)(2,1)S(1)} %bitcast.21, bf16[3,384,512]{2,1,0:T(8,128)(2,1)S(1)} %copy-done.2), kind=kOutput, calls=%fused_computation.4 | convolution fusion | flops 805306368 | bytes 6160384 | tf_op jit(solution)/shard_map/dot_general | solution.py:24
  83.7 0.0 copy-done.1
  83.7 0.0 copy-start.3
  83.7 3.3 %fusion = f32[512,2048]{1,0:T(8,128)} fusion(bf16[384,2048]{1,0:T(8,128)(2,1)S(1)} %bitcast.22, bf16[3,384,512]{2,1,0:T(8,128)(2,1)S(1)} %copy-done.2), kind=kOutput, calls=%fused_computation | convolution fusion | flops 805306368 | bytes 6160384 | tf_op jit(solution)/shard_map/dot_general | solution.py:24
  87.0 0.0 collective-permute-done
  87.0 3.5 %collective-permute-done.2 = bf16[192,512]{1,0:T(8,128)(2,1)S(1)} collective-permute-done((bf16[192,512]{1,0:T(8,128)(2,1)S(1)}, bf16[192,512]{1,0:T(8,128)(2,1)S(1)}, u32[]{:S(2)}, u32[]{:S(2)}) %collective-permute-start.2) | collective-permute-done | bytes 196640 | tf_op jit(solution)/shard_map/ppermute | solution.py:16
  90.5 0.0 collective-permute-done.1
  90.5 0.0 copy-done.3
  90.6 0.8 add_convert_fusion
Async XLA Ops:
  63.0 24.0 %collective-permute-start = (bf16[192,512]{1,0:T(8,128)(2,1)S(1)}, bf16[192,512]{1,0:T(8,128)(2,1)S(1)}, u32[]{:S(2)}, u32[]{:S(2)}) collective-permute-start(bf16[192,512]{1,0:T(8,128)(2,1)S(1)} %get-tuple-element.14), channel_id=1, source_target_pairs={{0,12},{4,0},{8,4},{12,8},{1,13},{5,1},{9,5},{13,9},{2,14},{6,2},{... | collective-permute-start | bytes 589832 | tf_op jit(solution)/shard_map/ppermute | solution.py:16
  74.8 15.7 %collective-permute-start.2 = (bf16[192,512]{1,0:T(8,128)(2,1)S(1)}, bf16[192,512]{1,0:T(8,128)(2,1)S(1)}, u32[]{:S(2)}, u32[]{:S(2)}) collective-permute-start(bf16[192,512]{1,0:T(8,128)(2,1)S(1)} %get-tuple-element.15), channel_id=1, source_target_pairs={{0,8},{4,12},{8,0},{12,4},{1,9},{5,13},{9,1},{13,5},{2,10},{6,14},... | collective-permute-start | bytes 589832 | tf_op jit(solution)/shard_map/ppermute | solution.py:16
  74.8 15.7 %collective-permute-start.1 = (bf16[192,512]{1,0:T(8,128)(2,1)S(1)}, bf16[192,512]{1,0:T(8,128)(2,1)S(1)}, u32[]{:S(2)}, u32[]{:S(2)}) collective-permute-start(bf16[192,512]{1,0:T(8,128)(2,1)S(1)} %get-tuple-element.16), channel_id=1, source_target_pairs={{0,4},{4,8},{8,12},{12,0},{1,5},{5,9},{9,13},{13,1},{2,6},{6,10},{... | collective-permute-start | bytes 589832 | tf_op jit(solution)/shard_map/ppermute | solution.py:16
  75.5 5.0 %copy-start = (bf16[2,192,2048]{2,1,0:T(8,128)(2,1)S(1)}, bf16[2,192,2048]{2,1,0:T(8,128)(2,1)}, u32[]{:S(2)}) copy-start(bf16[2,192,2048]{2,1,0:T(8,128)(2,1)} %get-tuple-element.12) | copy-start | bytes 4718596
  75.5 5.0 %copy-start.2 = (bf16[3,384,512]{2,1,0:T(8,128)(2,1)S(1)}, bf16[3,384,512]{2,1,0:T(8,128)(2,1)}, u32[]{:S(2)}) copy-start(bf16[3,384,512]{2,1,0:T(8,128)(2,1)} %get-tuple-element.11) | copy-start | bytes 3538948
  80.4 3.3 %copy-start.1 = (bf16[2,192,2048]{2,1,0:T(8,128)(2,1)S(1)}, bf16[2,192,2048]{2,1,0:T(8,128)(2,1)}, u32[]{:S(2)}) copy-start(bf16[2,192,2048]{2,1,0:T(8,128)(2,1)} %get-tuple-element.13) | copy-start | bytes 4718596
  83.7 6.8 %copy-start.3 = (f32[192,512]{1,0:T(8,128)S(1)}, f32[192,512]{1,0:T(8,128)}, u32[]{:S(2)}) copy-start(f32[192,512]{1,0:T(8,128)} %get-tuple-element.9) | copy-start | bytes 1179652
